TPU v7x, 512 devices: a whole 4x4x16 slice. The times are simulated.
512 devices in a mesh: stab: 16 (over z), round: 8 (over y, x_lo), shot: 4 (over x_hi, core).
Axes of the slice: x: 4 (x_hi: 2, x_lo: 2; x = x_hi * 2 + x_lo), y: 4, z: 16, core: 2. Of those that a mesh axis runs over, the one named last changes fastest.
Arguments:
- states_in: bfloat16 [8, 64, 624, 256], P('shot', 'round', 'stab'), parts along dimension 0, may hold values from -6 to 6
- bits: int32 [8, 64, 624], P('shot', 'round', 'stab'), parts along dimension 0, may hold values 0 or 1
- coords: int32 [64, 624], P('round', 'stab'), may hold values from 0 to 624
- coord_table: bfloat16 [625, 256], replicated, may hold values from -8 to 8
- flip_embed: bfloat16 [256], replicated, may hold values from -6 to 6
- gain_attn: bfloat16 [256], replicated, may hold values from 0.25 to 1.75
- w_query: bfloat16 [256, 256], replicated, may hold values from -1 to 1
- w_key: bfloat16 [256, 256], replicated, may hold values from -1 to 1
- w_value: bfloat16 [256, 256], replicated, may hold values from -0.375 to 0.375
- w_out: bfloat16 [256, 256], replicated, may hold values from -0.375 to 0.375
- gain_rec: bfloat16 [256], replicated, may hold values from 0.25 to 1.75
- w_decay: bfloat16 [256, 256], replicated, may hold values from -0.375 to 0.375
- decay_bias: float32 [256], replicated, may hold values from -1 to 6
- w_input: bfloat16 [256, 256], replicated, may hold values from -0.375 to 0.375
- w_rec_out: bfloat16 [256, 256], replicated, may hold values from -0.375 to 0.375
- gain_mlp: bfloat16 [256], replicated, may hold values from 0.25 to 1.75
- w_gate: bfloat16 [256, 1024], replicated, may hold values from -0.375 to 0.375
- w_up: bfloat16 [256, 1024], replicated, may hold values from -0.375 to 0.375
- w_down: bfloat16 [1024, 256], replicated, may hold values from -0.1875 to 0.1875
Outputs:
- states: bfloat16 [8, 64, 624, 256], P('shot', 'round', 'stab'), parts along dimension 0
There are 4 independent parts, one for each index of `shot`. A program takes and returns all parts, laid end to end along the dimension named above; an argument that names none is the same for every part. Nothing has to cross between parts.
All inputs are finite; a program needn't handle non-finite values. No bound on the sum of `bits` on one device may be relied on, other than what follows from the above.
Results may differ from a plain program's by a relative error of at most 0.0065.
Values may be sent and summed in bfloat16 or wider, within the bound.
A program may use at most 128 MiB of HBM per device.

v0:
```python
import jax
import jax.numpy as jnp
from jax import lax
from jax.sharding import PartitionSpec as P

HD = 32


def shifted(value, axis, steps):
    count = lax.axis_size(axis)
    initial, last = (max(0, -steps), min(count, count - steps))
    return lax.ppermute(value, axis, [(source, source + steps) for source in range(initial, last)])


def norm_rows(values, gain):
    scale = lax.rsqrt(jnp.mean(values * values, axis=-1, keepdims=True) + 1e-05)
    return (values * scale * gain.astype(jnp.float32)).astype(jnp.bfloat16)


def project(left, right):
    return jnp.dot(left, right, preferred_element_type=jnp.float32)


def softmax_step(carry, query, key_piece, value_piece):
    run_max, run_total, run_acc = carry
    scores = jnp.einsum(
        "brqhe,brkhe->brhqk", query, key_piece, preferred_element_type=jnp.float32
    ) * HD ** (-0.5)
    new_max = jnp.maximum(run_max, jnp.max(scores, axis=-1))
    expo = jnp.exp(scores - new_max[..., None])
    run_total = jnp.sum(expo, axis=-1)
    product = jnp.einsum(
        "brhqk,brkhe->brqhe",
        expo.astype(jnp.bfloat16),
        value_piece,
        preferred_element_type=jnp.float32,
    )
    run_acc = product
    return (new_max, run_total, run_acc)


def body(
    states_in,
    bits,
    coords,
    coord_table,
    flip_embed,
    gain_attn,
    w_query,
    w_key,
    w_value,
    w_out,
    gain_rec,
    w_decay,
    decay_bias,
    w_input,
    w_rec_out,
    gain_mlp,
    w_gate,
    w_up,
    w_down,
):
    shots, rounds, stabs = bits.shape
    width = coord_table.shape[1]
    heads = width // HD
    base = jnp.take(coord_table, coords, axis=0).astype(jnp.float32)
    signs = (2 * bits - 1).astype(jnp.float32)[..., None]
    start = states_in.astype(jnp.float32) + base[None] + signs * flip_embed.astype(jnp.float32)
    normed = norm_rows(start, gain_attn)
    query = project(normed, w_query).astype(jnp.bfloat16).reshape(shots, rounds, stabs, heads, HD)
    first_max = jnp.full((shots, rounds, heads, stabs), -1e30, jnp.float32)
    first_total = jnp.zeros((shots, rounds, heads, stabs), jnp.float32)
    first_acc = jnp.zeros((shots, rounds, stabs, heads, HD), jnp.float32)
    initial = (first_max, first_total, first_acc)
    keys = project(normed, w_key).astype(jnp.bfloat16)
    values = project(normed, w_value).astype(jnp.bfloat16)
    pieces = (
        lax.all_gather(keys, "stab", axis=2, tiled=True),
        lax.all_gather(values, "stab", axis=2, tiled=True),
    )
    count = pieces[0].shape[2]
    key_piece = pieces[0].reshape(shots, rounds, count, heads, HD)
    value_piece = pieces[1].reshape(shots, rounds, count, heads, HD)
    result = softmax_step(initial, query, key_piece, value_piece)
    final_total = jnp.transpose(result[1], (0, 1, 3, 2))[..., None]
    mixed = (result[2] / final_total).astype(jnp.bfloat16).reshape(shots, rounds, stabs, width)
    after_attn = start + project(mixed, w_out)
    rec_in = norm_rows(after_attn, gain_rec)
    decay = jax.nn.sigmoid(project(rec_in, w_decay) + decay_bias)
    drive = (1.0 - decay) * project(rec_in, w_input)

    def advance(state, inputs):
        local_state, product = state
        local_state = inputs[0] * local_state + inputs[1]
        product = product * inputs[0]
        return ((local_state, product), (local_state, product))

    zero_state = jnp.zeros((shots, stabs, width), jnp.float32)
    unit_state = jnp.ones((shots, stabs, width), jnp.float32)
    ending, history = lax.scan(
        advance, (zero_state, unit_state), (jnp.moveaxis(decay, 1, 0), jnp.moveaxis(drive, 1, 0))
    )
    last_state, last_product = ending

    def relay_step(step, entering):
        return shifted(
            (last_product * entering + last_state).astype(jnp.bfloat16), "round", 1
        ).astype(jnp.float32)

    incoming = lax.fori_loop(0, lax.axis_size("round") - 1, relay_step, zero_state)
    hidden = history[0] + history[1] * incoming[None]
    hidden = jnp.moveaxis(hidden, 0, 1)
    after_rec = after_attn + project(hidden.astype(jnp.bfloat16), w_rec_out)
    ffn_in = norm_rows(after_rec, gain_mlp)
    inner = (jax.nn.silu(project(ffn_in, w_gate)) * project(ffn_in, w_up)).astype(jnp.bfloat16)
    return (after_rec + project(inner, w_down)).astype(jnp.bfloat16)


def solution(mesh):
    placed = (
        P("shot", "round", "stab", None),
        P("shot", "round", "stab"),
        P("round", "stab"),
        P(),
        P(),
        P(),
        P(),
        P(),
        P(),
        P(),
        P(),
        P(),
        P(),
        P(),
        P(),
        P(),
        P(),
        P(),
        P(),
    )
    return jax.shard_map(
        body,
        mesh=mesh,
        in_specs=placed,
        out_specs=P("shot", "round", "stab", None),
        check_vma=False,
    )
```

profile of v0, /device:TPU:8, one launch (start us, length us, event | category | flops | bytes accessed | tf_op | source)
XLA Modules:
  0.0 271.6 jit_solution(17156289981482771715)
XLA Ops:
  8.1 2.6 gather_fusion
  12.3 1.3 multiply_reduce_fusion.3
  14.3 1.2 multiply_convert_fusion.3
  15.5 1.1 convolution_convert_fusion
  19.4 83.3 %all-gather.5.cloned.1.call-done = bf16[2,8,624,256]{3,1,0,2:T(8,128)(2,1)} async-done(((bf16[2,8,39,256]{3,1,0,2:T(8,128)(2,1)}), bf16[2,8,624,256]{3,1,0,2:T(8,128)(2,1)}) %all-gather.5.cloned.1.call-update) | async-done | bytes 5111824 | tf_op jit(solution)/shard_map/all_gather | solution.py:78
  102.7 8.9 %copy.44 = bf16[2,8,624,256]{2,3,1,0:T(8,128)(2,1)} copy(bf16[2,8,624,256]{3,1,0,2:T(8,128)(2,1)} %all-gather.5.cloned.1.call-done) | data formatting | bytes 10223616 | tf_op jit(solution)/shard_map/all_gather | solution.py:78
  111.6 4.4 %multiply_reduce_fusion = (f32[2,8,8,39]{3,2,1,0:T(8,128)S(1)}, f32[2,8,8,39,624]{4,3,2,1,0:T(8,128)S(1)}) fusion(bf16[2,8,39,8,32]{2,4,3,1,0:T(8,128)(2,1)S(1)} %bitcast.103, bf16[2,8,624,8,32]{2,4,3,1,0:T(8,128)(2,1)} %bitcast.101), kind=kOutput, calls=%fused_computation.10 | convolution fusion | flops 205585536 | bytes 17911296 | tf_op jit(solution)/shard_map/brqhe,brkhe->brhqk/dot_general | solution.py:26
  116.1 4.7 %copy-done.1 = f32[2,8,8,39,624]{4,3,2,1,0:T(8,128)} copy-done((f32[2,8,8,39,624]{4,3,2,1,0:T(8,128)}, f32[2,8,8,39,624]{4,3,2,1,0:T(8,128)S(1)}, u32[]{:S(2)}) %copy-start.1) | copy-done | bytes 12460056
  120.7 3.3 %fusion.2 = f32[2,8,8,39]{3,2,1,0:T(8,128)S(1)} fusion(f32[2,8,8,39,624]{4,3,2,1,0:T(8,128)S(1)} %get-tuple-element.161, f32[2,8,8,39]{3,2,1,0:T(8,128)S(1)} %broadcast_maximum_fusion), kind=kLoop, calls=%fused_computation.11 | loop fusion | flops 9340032 | bytes 12499968 | tf_op jit(solution)/shard_map/reduce_sum | solution.py:31
  124.0 57.4 %all-gather.3.cloned.1.call-done = bf16[2,8,624,256]{3,1,0,2:T(8,128)(2,1)} async-done(((bf16[2,8,39,256]{3,1,0,2:T(8,128)(2,1)}), bf16[2,8,624,256]{3,1,0,2:T(8,128)(2,1)}) %all-gather.3.cloned.1.call-update) | async-done | bytes 5111824 | tf_op jit(solution)/shard_map/all_gather | solution.py:79
  181.5 8.9 %copy.41 = bf16[2,8,624,256]{2,3,1,0:T(8,128)(2,1)} copy(bf16[2,8,624,256]{3,1,0,2:T(8,128)(2,1)} %all-gather.3.cloned.1.call-done) | data formatting | bytes 10223616 | tf_op jit(solution)/shard_map/all_gather | solution.py:79
  190.4 10.0 %fusion.8 = bf16[2,8,39,8,32]{2,4,3,1,0:T(8,128)(2,1)} fusion(bf16[2,8,624,8,32]{2,4,3,1,0:T(8,128)(2,1)} %bitcast.102, f32[2,8,8,39,624]{4,3,2,1,0:T(8,128)} %copy-done.1, f32[2,8,8,39]{3,2,1,0:T(8,128)S(1)} %broadcast_maximum_fusion, f32[2,8,39,8]{2,3,1,0:T(8,128)S(1)} %bitcast.105), kind=kOutput, calls=%fused_computation.18 | convolution fusion | flops 209025024 | bytes 17931264 | tf_op jit(solution)/shard_map/brhqk,brkhe->brqhe/dot_general | solution.py:32
  200.3 1.9 multiply_reduce_fusion.2
  203.0 5.5 %while.28 = (s32[]{:T(128)}, f32[2,39,256]{2,1,0:T(8,128)S(1)}, f32[2,39,256]{2,1,0:T(8,128)S(1)}, f32[8,2,39,256]{3,2,1,0:T(8,128)S(1)}, f32[8,2,39,256]{3,2,1,...) while((s32[]{:T(128)}, f32[2,39,256]{2,1,0:T(8,128)S(1)}, ...), condition=%wide.region_5.6_spmd.clone, body=%wide.region_4.5_spmd.clone.sunk | while | flops 99843 | bytes 655975 | solution.py:100
  208.5 48.2 %while.29 = (s32[]{:T(128)}, f32[2,39,256]{2,1,0:T(8,128)S(1)}, f32[2,39,256]{2,1,0:T(8,128)S(1)}, f32[2,39,256]{2,1,0:T(8,128)S(1)}, s32[]{:T(128)}, /*index=5*/s32[]{:T(128)}) while((s32[]{:T(128)}, f32[2,39,256]{2,1,0:T(8,128)S(1)}, f32[2,39,256]{2,1,0:T(8,128)S(1)}, f32[2,39,256]{2,1,0:T(8,128)S(1)}, s32[]{:T(128)}, ...), condition=%wide.region_7.8_spmd.clone, body=%wide.region_6.7_spmd.clone.sunk | while | flops 99843 | bytes 559223 | solution.py:110
  208.5 3.3 %collective-permute-start = (bf16[2,39,256]{2,1,0:T(8,128)(2,1)S(1)}, bf16[2,39,256]{2,1,0:T(8,128)(2,1)S(1)}, u32[]{:S(2)}, u32[]{:S(2)}) collective-permute-start(bf16[2,39,256]{2,1,0:T(8,128)(2,1)S(1)} %fusion.50), channel_id=1, source_target_pairs={{0,4},{4,8},{8,12},{12,16},{16,20},{20,24},{24,28},{1,5},{5,9},{9,... | collective-permute-start | bytes 119816 | tf_op jit(solution)/shard_map/while/body/eval_jaxpr/ppermute | solution.py:12
  211.8 3.5 %collective-permute-done = bf16[2,39,256]{2,1,0:T(8,128)(2,1)S(1)} collective-permute-done((bf16[2,39,256]{2,1,0:T(8,128)(2,1)S(1)}, bf16[2,39,256]{2,1,0:T(8,128)(2,1)S(1)}, u32[]{:S(2)}, u32[]{:S(2)}) %collective-permute-start) | collective-permute-done | bytes 39968 | tf_op jit(solution)/shard_map/while/body/eval_jaxpr/ppermute | solution.py:12
  215.4 2.4 collective-permute-start
  217.7 4.4 %collective-permute-done = bf16[2,39,256]{2,1,0:T(8,128)(2,1)S(1)} collective-permute-done((bf16[2,39,256]{2,1,0:T(8,128)(2,1)S(1)}, bf16[2,39,256]{2,1,0:T(8,128)(2,1)S(1)}, u32[]{:S(2)}, u32[]{:S(2)}) %collective-permute-start) | collective-permute-done | bytes 39968 | tf_op jit(solution)/shard_map/while/body/eval_jaxpr/ppermute | solution.py:12
  222.2 1.9 collective-permute-start
  224.1 4.9 %collective-permute-done = bf16[2,39,256]{2,1,0:T(8,128)(2,1)S(1)} collective-permute-done((bf16[2,39,256]{2,1,0:T(8,128)(2,1)S(1)}, bf16[2,39,256]{2,1,0:T(8,128)(2,1)S(1)}, u32[]{:S(2)}, u32[]{:S(2)}) %collective-permute-start) | collective-permute-done | bytes 39968 | tf_op jit(solution)/shard_map/while/body/eval_jaxpr/ppermute | solution.py:12
  229.1 1.9 collective-permute-start
  231.0 5.2 %collective-permute-done = bf16[2,39,256]{2,1,0:T(8,128)(2,1)S(1)} collective-permute-done((bf16[2,39,256]{2,1,0:T(8,128)(2,1)S(1)}, bf16[2,39,256]{2,1,0:T(8,128)(2,1)S(1)}, u32[]{:S(2)}, u32[]{:S(2)}) %collective-permute-start) | collective-permute-done | bytes 39968 | tf_op jit(solution)/shard_map/while/body/eval_jaxpr/ppermute | solution.py:12
  236.2 1.9 collective-permute-start
  238.2 4.9 %collective-permute-done = bf16[2,39,256]{2,1,0:T(8,128)(2,1)S(1)} collective-permute-done((bf16[2,39,256]{2,1,0:T(8,128)(2,1)S(1)}, bf16[2,39,256]{2,1,0:T(8,128)(2,1)S(1)}, u32[]{:S(2)}, u32[]{:S(2)}) %collective-permute-start) | collective-permute-done | bytes 39968 | tf_op jit(solution)/shard_map/while/body/eval_jaxpr/ppermute | solution.py:12
  243.1 1.9 collective-permute-start
  245.0 4.9 %collective-permute-done = bf16[2,39,256]{2,1,0:T(8,128)(2,1)S(1)} collective-permute-done((bf16[2,39,256]{2,1,0:T(8,128)(2,1)S(1)}, bf16[2,39,256]{2,1,0:T(8,128)(2,1)S(1)}, u32[]{:S(2)}, u32[]{:S(2)}) %collective-permute-start) | collective-permute-done | bytes 39968 | tf_op jit(solution)/shard_map/while/body/eval_jaxpr/ppermute | solution.py:12
  249.9 1.9 collective-permute-start
  251.8 4.9 %collective-permute-done = bf16[2,39,256]{2,1,0:T(8,128)(2,1)S(1)} collective-permute-done((bf16[2,39,256]{2,1,0:T(8,128)(2,1)S(1)}, bf16[2,39,256]{2,1,0:T(8,128)(2,1)S(1)}, u32[]{:S(2)}, u32[]{:S(2)}) %collective-permute-start) | collective-permute-done | bytes 39968 | tf_op jit(solution)/shard_map/while/body/eval_jaxpr/ppermute | solution.py:12
  256.7 1.4 multiply_reduce_fusion.1
  259.6 3.4 %fusion.17 = bf16[2,8,39,256]{3,2,1,0:T(8,128)(2,1)} fusion(f32[2,8,39,256]{3,2,1,0:T(8,128)} %copy-done.3, f32[2,8,39,1024]{3,2,1,0:T(8,128)S(1)} %fusion.21, bf16[1024,256]{1,0:T(8,128)(2,1)} %param.41, bf16[256,1024]{1,0:T(8,128)(2,1)} %param.40, f32[256]{0:T(256)S(1)} %convert_element_type.82, f32[2,8,39]{2,1,0:T(8,128)S(1)} %add_rsqrt_fusion), kind=kOutput, calls=%fused_computation.30 | convolution fusion | flops 658944000 | bytes 4566464 | tf_op jit(solution)/shard_map/dot_general | solution.py:21
  263.0 1.8 copy.50
  (77 shorter events, 14.3 us)
Async XLA Ops:
  6.5 252.5 %copy-start = (bf16[256,1024]{1,0:T(8,128)(2,1)S(1)}, bf16[256,1024]{1,0:T(8,128)(2,1)}, u32[]{:S(2)}) copy-start(bf16[256,1024]{1,0:T(8,128)(2,1)} %param.39) | copy-start | bytes 1572868
  6.5 11.0 %copy-start.5 = (bf16[256,256]{1,0:T(8,128)(2,1)S(1)}, bf16[256,256]{1,0:T(8,128)(2,1)}, u32[]{:S(2)}) copy-start(bf16[256,256]{1,0:T(8,128)(2,1)} %param.31) | copy-start | bytes 393220
  6.5 12.1 %copy-start.6 = (bf16[256,256]{1,0:T(8,128)(2,1)S(1)}, bf16[256,256]{1,0:T(8,128)(2,1)}, u32[]{:S(2)}) copy-start(bf16[256,256]{1,0:T(8,128)(2,1)} %param.29) | copy-start | bytes 393220
  6.5 12.9 %copy-start.10 = (bf16[256]{0:T(256)(128)(2,1)S(1)}, bf16[256]{0:T(256)(128)(2,1)}, u32[]{:S(2)}) copy-start(bf16[256]{0:T(256)(128)(2,1)} %param.33) | copy-start | bytes 1540
  6.5 12.9 %copy-start.11 = (bf16[256]{0:T(256)(128)(2,1)S(1)}, bf16[256]{0:T(256)(128)(2,1)}, u32[]{:S(2)}) copy-start(bf16[256]{0:T(256)(128)(2,1)} %param.38) | copy-start | bytes 1540
  6.5 96.2 %all-gather.5.cloned.1.call-start = ((), (), s32[]{:S(2)}) async-start(), calls=%async_computation.1 | async-start | bytes 5431296 | tf_op jit(solution)/shard_map/all_gather | solution.py:78
  17.5 164.0 %all-gather.3.cloned.1.call-start = ((), (), s32[]{:S(2)}) async-start(), calls=%async_computation | async-start | bytes 5431296 | tf_op jit(solution)/shard_map/all_gather | solution.py:79
  116.0 4.7 %copy-start.1 = (f32[2,8,8,39,624]{4,3,2,1,0:T(8,128)}, f32[2,8,8,39,624]{4,3,2,1,0:T(8,128)S(1)}, u32[]{:S(2)}) copy-start(f32[2,8,8,39,624]{4,3,2,1,0:T(8,128)S(1)} %get-tuple-element.161) | copy-start | bytes 37380100
  190.3 10.0 %copy-start.2 = (bf16[2,8,39,256]{3,1,2,0:T(8,128)(2,1)S(1)}, bf16[2,8,39,256]{3,1,2,0:T(8,128)(2,1)}, u32[]{:S(2)}) copy-start(bf16[2,8,39,256]{3,1,2,0:T(8,128)(2,1)} %param.23) | copy-start | bytes 958468
  190.3 10.0 %copy-start.4 = (bf16[256,256]{1,0:T(8,128)(2,1)S(1)}, bf16[256,256]{1,0:T(8,128)(2,1)}, u32[]{:S(2)}) copy-start(bf16[256,256]{1,0:T(8,128)(2,1)} %param.32) | copy-start | bytes 393220
  190.3 11.8 %copy-start.8 = (bf16[256,256]{1,0:T(8,128)(2,1)S(1)}, bf16[256,256]{1,0:T(8,128)(2,1)}, u32[]{:S(2)}) copy-start(bf16[256,256]{1,0:T(8,128)(2,1)} %param.34) | copy-start | bytes 393220
  190.3 11.9 %copy-start.9 = (f32[256]{0:T(256)S(1)}, f32[256]{0:T(256)}, u32[]{:S(2)}) copy-start(f32[256]{0:T(256)} %param.35) | copy-start | bytes 3076
  200.3 2.3 copy-start.7
  208.5 6.8 %collective-permute-start = (bf16[2,39,256]{2,1,0:T(8,128)(2,1)S(1)}, bf16[2,39,256]{2,1,0:T(8,128)(2,1)S(1)}, u32[]{:S(2)}, u32[]{:S(2)}) collective-permute-start(bf16[2,39,256]{2,1,0:T(8,128)(2,1)S(1)} %fusion.50), channel_id=1, source_target_pairs={{0,4},{4,8},{8,12},{12,16},{16,20},{20,24},{24,28},{1,5},{5,9},{9,... | collective-permute-start | bytes 119816 | tf_op jit(solution)/shard_map/while/body/eval_jaxpr/ppermute | solution.py:12
  215.4 6.8 %collective-permute-start = (bf16[2,39,256]{2,1,0:T(8,128)(2,1)S(1)}, bf16[2,39,256]{2,1,0:T(8,128)(2,1)S(1)}, u32[]{:S(2)}, u32[]{:S(2)}) collective-permute-start(bf16[2,39,256]{2,1,0:T(8,128)(2,1)S(1)} %fusion.50), channel_id=1, source_target_pairs={{0,4},{4,8},{8,12},{12,16},{16,20},{20,24},{24,28},{1,5},{5,9},{9,... | collective-permute-start | bytes 119816 | tf_op jit(solution)/shard_map/while/body/eval_jaxpr/ppermute | solution.py:12
  222.2 6.8 %collective-permute-start = (bf16[2,39,256]{2,1,0:T(8,128)(2,1)S(1)}, bf16[2,39,256]{2,1,0:T(8,128)(2,1)S(1)}, u32[]{:S(2)}, u32[]{:S(2)}) collective-permute-start(bf16[2,39,256]{2,1,0:T(8,128)(2,1)S(1)} %fusion.50), channel_id=1, source_target_pairs={{0,4},{4,8},{8,12},{12,16},{16,20},{20,24},{24,28},{1,5},{5,9},{9,... | collective-permute-start | bytes 119816 | tf_op jit(solution)/shard_map/while/body/eval_jaxpr/ppermute | solution.py:12
  229.1 7.1 %collective-permute-start = (bf16[2,39,256]{2,1,0:T(8,128)(2,1)S(1)}, bf16[2,39,256]{2,1,0:T(8,128)(2,1)S(1)}, u32[]{:S(2)}, u32[]{:S(2)}) collective-permute-start(bf16[2,39,256]{2,1,0:T(8,128)(2,1)S(1)} %fusion.50), channel_id=1, source_target_pairs={{0,4},{4,8},{8,12},{12,16},{16,20},{20,24},{24,28},{1,5},{5,9},{9,... | collective-permute-start | bytes 119816 | tf_op jit(solution)/shard_map/while/body/eval_jaxpr/ppermute | solution.py:12
  236.2 6.8 %collective-permute-start = (bf16[2,39,256]{2,1,0:T(8,128)(2,1)S(1)}, bf16[2,39,256]{2,1,0:T(8,128)(2,1)S(1)}, u32[]{:S(2)}, u32[]{:S(2)}) collective-permute-start(bf16[2,39,256]{2,1,0:T(8,128)(2,1)S(1)} %fusion.50), channel_id=1, source_target_pairs={{0,4},{4,8},{8,12},{12,16},{16,20},{20,24},{24,28},{1,5},{5,9},{9,... | collective-permute-start | bytes 119816 | tf_op jit(solution)/shard_map/while/body/eval_jaxpr/ppermute | solution.py:12
  243.1 6.8 %collective-permute-start = (bf16[2,39,256]{2,1,0:T(8,128)(2,1)S(1)}, bf16[2,39,256]{2,1,0:T(8,128)(2,1)S(1)}, u32[]{:S(2)}, u32[]{:S(2)}) collective-permute-start(bf16[2,39,256]{2,1,0:T(8,128)(2,1)S(1)} %fusion.50), channel_id=1, source_target_pairs={{0,4},{4,8},{8,12},{12,16},{16,20},{20,24},{24,28},{1,5},{5,9},{9,... | collective-permute-start | bytes 119816 | tf_op jit(solution)/shard_map/while/body/eval_jaxpr/ppermute | solution.py:12
  249.9 6.8 %collective-permute-start = (bf16[2,39,256]{2,1,0:T(8,128)(2,1)S(1)}, bf16[2,39,256]{2,1,0:T(8,128)(2,1)S(1)}, u32[]{:S(2)}, u32[]{:S(2)}) collective-permute-start(bf16[2,39,256]{2,1,0:T(8,128)(2,1)S(1)} %fusion.50), channel_id=1, source_target_pairs={{0,4},{4,8},{8,12},{12,16},{16,20},{20,24},{24,28},{1,5},{5,9},{9,... | collective-permute-start | bytes 119816 | tf_op jit(solution)/shard_map/while/body/eval_jaxpr/ppermute | solution.py:12
  258.2 0.8 copy-start.3
Sparse Core Ops, SparseCore 0:
  17.6 85.0 all-gather.4
  104.8 76.6 all-gather.2
where the time goes:
time: 273 us; the launch traced here: 272 us
  waiting for transfers between devices  173 us (63%)
  local copies, waits for them, and re-layouts  29.9 us (11%)
  matrix products  24 us (9%)
  starting transfers between devices  15.3 us (6%)
  other arithmetic  15.1 us (6%)
  between operations  13.7 us (5%)
    all_gather x1, waiting for transfers between devices, body(): lax.all_gather(keys, 'stab', axis=2, tiled=True)  83.3 us
    all_gather x1, waiting for transfers between devices, body(): lax.all_gather(values, 'stab', axis=2, tiled=True)  57.4 us
    ppermute x7, waiting for transfers between devices, shifted(): lax.ppermute(value, axis, [(source, source + steps) for source in range(i...  32.6 us
    ppermute x7, starting transfers between devices, shifted(): lax.ppermute(value, axis, [(source, source + steps) for source in range(i...  15.2 us
    dot_general x1, matrix products, softmax_step(): jnp.einsum('brhqk,brkhe->brqhe', expo.astype(jnp.bfloat16), value_piece,...  9.95 us
    dot_general x9, matrix products, project(): return jnp.dot(left, right, preferred_element_type=jnp.float32)  9.63 us
    all_gather x1, local copies, waits for them, and re-layouts, body(): lax.all_gather(keys, 'stab', axis=2, tiled=True)  8.89 us
    all_gather x1, local copies, waits for them, and re-layouts, body(): lax.all_gather(values, 'stab', axis=2, tiled=True)  8.87 us
  transfers between devices with their start and end apart: 9, of which 9 were waited for; matrix products, arithmetic and copies ran while one was open for 7% of the time, Pallas kernels for 0%

commit v1 on v0

--- a/solution.py
+++ b/solution.py
@@ -76,7 +76,9 @@
     values = project(normed, w_value).astype(jnp.bfloat16)
     pieces = (
         lax.all_gather(keys, "stab", axis=2, tiled=True),
-        lax.all_gather(values, "stab", axis=2, tiled=True),
+        jnp.concatenate(
+            lax.all_to_all(jnp.stack([values] * lax.axis_size("stab")), "stab", 0, 0), axis=2
+        ),
     )
     count = pieces[0].shape[2]
     key_piece = pieces[0].reshape(shots, rounds, count, heads, HD)

time: 273 us -> 450 us (1.65)
  waiting for transfers between devices: 173 us -> 307 us
  local copies, waits for them, and re-layouts: 29.9 us -> 58.6 us
  starting transfers between devices: 15.3 us -> 31 us
    all_gather x1, waiting for transfers between devices: 83.3 us -> 274 us  [body(): lax.all_gather(keys, 'stab', axis=2, tiled=True)]
    all_gather x1 -> x0, waiting for transfers between devices: 57.4 us -> none  [body(): lax.all_gather(values, 'stab', axis=2, tiled=True)]
    another operation x0 -> x2, local copies, waits for them, and re-layouts: none -> 26.4 us  [the longest x1 23.7 us: body(): value_piece = pieces[1].reshape(shots, rounds, count, heads, HD)]
    all_to_all x0 -> x1, starting transfers between devices: none -> 15.4 us  [body(): lax.all_to_all(jnp.stack([values] * lax.axis_size('stab')), 'stab', 0, 0)]
    reshape x0 -> x1, local copies, waits for them, and re-layouts: none -> 12.9 us  [body(): jnp.concatenate(lax.all_to_all(jnp.stack([values] * lax.axis_size('stab')...]
    all_gather x1 -> x0, local copies, waits for them, and re-layouts: 8.87 us -> none  [body(): lax.all_gather(values, 'stab', axis=2, tiled=True)]
  transfers between devices with their start and end apart: 9 -> 9, of which waited for: 9 -> 8; matrix products, arithmetic and copies ran while one was open for 7% -> 4% of each run, Pallas kernels for 0% -> 0%
where the time goes in v1:
time: 450 us; the launch traced here: 449 us
  waiting for transfers between devices  307 us (68%)
  local copies, waits for them, and re-layouts  58.6 us (13%)
  starting transfers between devices  31 us (7%)
  matrix products  23.3 us (5%)
  other arithmetic  15.1 us (3%)
  between operations  13.7 us (3%)
    all_gather x1, waiting for transfers between devices, body(): lax.all_gather(keys, 'stab', axis=2, tiled=True)  274 us
    ppermute x7, waiting for transfers between devices, shifted(): lax.ppermute(value, axis, [(source, source + steps) for source in range(i...  32.4 us
    another operation x1, local copies, waits for them, and re-layouts, body(): value_piece = pieces[1].reshape(shots, rounds, count, heads, HD)  23.7 us
    ppermute x7, starting transfers between devices, shifted(): lax.ppermute(value, axis, [(source, source + steps) for source in range(i...  15.4 us
    all_to_all x1, starting transfers between devices, body(): lax.all_to_all(jnp.stack([values] * lax.axis_size('stab')), 'stab', 0, 0)  15.4 us
    reshape x1, local copies, waits for them, and re-layouts, body(): jnp.concatenate(lax.all_to_all(jnp.stack([values] * lax.axis_size('stab')...  12.9 us
    dot_general x1, matrix products, softmax_step(): jnp.einsum('brhqk,brkhe->brqhe', expo.astype(jnp.bfloat16), value_piece,...  9.94 us
  transfers between devices with their start and end apart: 9, of which 8 were waited for; matrix products, arithmetic and copies ran while one was open for 4% of the time, Pallas kernels for 0%

profile of v1, /device:TPU:8, one launch (start us, length us, event | category | flops | bytes accessed | tf_op | source)
XLA Modules:
  0.0 448.6 jit_solution(1586161048110741378)
XLA Ops:
  10.1 2.6 gather_fusion
  12.9 1.3 multiply_reduce_fusion.3
  14.2 1.2 multiply_convert_fusion.3
  16.7 2.6 stack.2
  19.3 15.4 %all-to-all-start = ((bf16[16,2,8,39,256]{4,2,3,1,0:T(8,128)(2,1)}), bf16[16,2,8,39,256]{4,2,3,1,0:T(8,128)(2,1)}, u32[]{:S(2)}, u32[]{:S(2)}) async-start(bf16[16,2,8,39,256]{4,2,3,1,0:T(8,128)(2,1)} %stack.2), calls=%async_computation | async-start | bytes 10223616 | tf_op jit(solution)/shard_map/all_to_all | solution.py:80
  36.8 274.1 %all-gather.2.cloned.1.call-done = bf16[2,8,624,256]{3,1,0,2:T(8,128)(2,1)} async-done(((bf16[2,8,39,256]{3,1,0,2:T(8,128)(2,1)}), bf16[2,8,624,256]{3,1,0,2:T(8,128)(2,1)}) %all-gather.2.cloned.1.call-update) | async-done | bytes 5111824 | tf_op jit(solution)/shard_map/all_gather | solution.py:78
  311.0 8.9 %copy.44 = bf16[2,8,624,256]{2,3,1,0:T(8,128)(2,1)} copy(bf16[2,8,624,256]{3,1,0,2:T(8,128)(2,1)} %all-gather.2.cloned.1.call-done) | data formatting | bytes 10223616 | tf_op jit(solution)/shard_map/all_gather | solution.py:78
  319.9 4.4 multiply_reduce_fusion
  324.3 4.7 %copy-done.1 = f32[2,8,8,39,624]{4,3,2,1,0:T(8,128)} copy-done((f32[2,8,8,39,624]{4,3,2,1,0:T(8,128)}, f32[2,8,8,39,624]{4,3,2,1,0:T(8,128)S(1)}, u32[]{:S(2)}) %copy-start.1) | copy-done | bytes 12460056
  329.0 3.3 fusion.2
  332.3 12.9 %copy.41 = bf16[2,8,16,39,256]{3,2,4,1,0:T(8,128)(2,1)} copy(bf16[2,8,16,39,256]{4,1,3,0,2:T(8,128)(2,1)} %bitcast.2) | data formatting | bytes 10223616 | tf_op jit(solution)/shard_map/reshape | solution.py:79
  345.2 23.7 %reshape_reshape.3 = bf16[2,8,624,8,32]{2,4,3,1,0:T(8,128)(2,1)} reshape(bf16[2,8,16,39,256]{3,2,4,1,0:T(8,128)(2,1)} %copy.41) | data formatting | bytes 10223616 | tf_op jit(solution)/shard_map/reshape;reshape | solution.py:85
  369.0 9.9 %fusion.8 = bf16[2,8,39,8,32]{2,4,3,1,0:T(8,128)(2,1)} fusion(bf16[2,8,624,8,32]{2,4,3,1,0:T(8,128)(2,1)} %reshape_reshape.3, f32[2,8,8,39,624]{4,3,2,1,0:T(8,128)} %copy-done.1, f32[2,8,8,39]{3,2,1,0:T(8,128)S(1)} %broadcast_maximum_fusion, f32[2,8,39,8]{2,3,1,0:T(8,128)S(1)} %bitcast.108), kind=kOutput, calls=%fused_computation.18 | convolution fusion | flops 209025024 | bytes 17931264 | tf_op jit(solution)/shard_map/brhqk,brkhe->brqhe/dot_general | solution.py:32
  378.9 1.9 multiply_reduce_fusion.2
  381.6 5.5 %while.28 = (s32[]{:T(128)}, f32[2,39,256]{2,1,0:T(8,128)S(1)}, f32[2,39,256]{2,1,0:T(8,128)S(1)}, f32[8,2,39,256]{3,2,1,0:T(8,128)S(1)}, f32[8,2,39,256]{3,2,1,...) while((s32[]{:T(128)}, f32[2,39,256]{2,1,0:T(8,128)S(1)}, ...), condition=%wide.region_5.6_spmd.clone, body=%wide.region_4.5_spmd.clone.sunk | while | flops 99843 | bytes 655475 | solution.py:102
  387.1 48.3 %while.29 = (s32[]{:T(128)}, f32[2,39,256]{2,1,0:T(8,128)S(1)}, f32[2,39,256]{2,1,0:T(8,128)S(1)}, f32[2,39,256]{2,1,0:T(8,128)S(1)}, s32[]{:T(128)}, /*index=5*/s32[]{:T(128)}) while((s32[]{:T(128)}, f32[2,39,256]{2,1,0:T(8,128)S(1)}, f32[2,39,256]{2,1,0:T(8,128)S(1)}, f32[2,39,256]{2,1,0:T(8,128)S(1)}, s32[]{:T(128)}, ...), condition=%wide.region_7.8_spmd.clone, body=%wide.region_6.7_spmd.clone.sunk | while | flops 99843 | bytes 559223 | solution.py:112
  387.1 3.4 collective-permute-start
  390.5 3.4 collective-permute-done
  394.0 2.5 collective-permute-start
  396.4 4.3 collective-permute-done
  400.8 1.9 collective-permute-start
  402.7 4.9 %collective-permute-done = bf16[2,39,256]{2,1,0:T(8,128)(2,1)S(1)} collective-permute-done((bf16[2,39,256]{2,1,0:T(8,128)(2,1)S(1)}, bf16[2,39,256]{2,1,0:T(8,128)(2,1)S(1)}, u32[]{:S(2)}, u32[]{:S(2)}) %collective-permute-start) | collective-permute-done | bytes 39968 | tf_op jit(solution)/shard_map/while/body/eval_jaxpr/ppermute | solution.py:12
  407.6 1.9 collective-permute-start
  409.6 5.2 %collective-permute-done = bf16[2,39,256]{2,1,0:T(8,128)(2,1)S(1)} collective-permute-done((bf16[2,39,256]{2,1,0:T(8,128)(2,1)S(1)}, bf16[2,39,256]{2,1,0:T(8,128)(2,1)S(1)}, u32[]{:S(2)}, u32[]{:S(2)}) %collective-permute-start) | collective-permute-done | bytes 39968 | tf_op jit(solution)/shard_map/while/body/eval_jaxpr/ppermute | solution.py:12
  414.9 1.9 collective-permute-start
  416.8 4.9 %collective-permute-done = bf16[2,39,256]{2,1,0:T(8,128)(2,1)S(1)} collective-permute-done((bf16[2,39,256]{2,1,0:T(8,128)(2,1)S(1)}, bf16[2,39,256]{2,1,0:T(8,128)(2,1)S(1)}, u32[]{:S(2)}, u32[]{:S(2)}) %collective-permute-start) | collective-permute-done | bytes 39968 | tf_op jit(solution)/shard_map/while/body/eval_jaxpr/ppermute | solution.py:12
  421.7 1.9 collective-permute-start
  423.6 4.9 %collective-permute-done = bf16[2,39,256]{2,1,0:T(8,128)(2,1)S(1)} collective-permute-done((bf16[2,39,256]{2,1,0:T(8,128)(2,1)S(1)}, bf16[2,39,256]{2,1,0:T(8,128)(2,1)S(1)}, u32[]{:S(2)}, u32[]{:S(2)}) %collective-permute-start) | collective-permute-done | bytes 39968 | tf_op jit(solution)/shard_map/while/body/eval_jaxpr/ppermute | solution.py:12
  428.6 1.9 collective-permute-start
  430.5 4.9 %collective-permute-done = bf16[2,39,256]{2,1,0:T(8,128)(2,1)S(1)} collective-permute-done((bf16[2,39,256]{2,1,0:T(8,128)(2,1)S(1)}, bf16[2,39,256]{2,1,0:T(8,128)(2,1)S(1)}, u32[]{:S(2)}, u32[]{:S(2)}) %collective-permute-start) | collective-permute-done | bytes 39968 | tf_op jit(solution)/shard_map/while/body/eval_jaxpr/ppermute | solution.py:12
  435.4 1.5 multiply_reduce_fusion.1
  438.2 2.7 fusion.17
  (78 shorter events, 15.6 us)
Async XLA Ops:
  6.5 431.1 %copy-start = (bf16[256,1024]{1,0:T(8,128)(2,1)S(1)}, bf16[256,1024]{1,0:T(8,128)(2,1)}, u32[]{:S(2)}) copy-start(bf16[256,1024]{1,0:T(8,128)(2,1)} %param.39) | copy-start | bytes 1572868
  19.3 15.6 %copy-start.5 = (bf16[256,256]{1,0:T(8,128)(2,1)S(1)}, bf16[256,256]{1,0:T(8,128)(2,1)}, u32[]{:S(2)}) copy-start(bf16[256,256]{1,0:T(8,128)(2,1)} %param.30) | copy-start | bytes 393220
  19.3 16.7 %copy-start.6 = (bf16[256,256]{1,0:T(8,128)(2,1)S(1)}, bf16[256,256]{1,0:T(8,128)(2,1)}, u32[]{:S(2)}) copy-start(bf16[256,256]{1,0:T(8,128)(2,1)} %param.29) | copy-start | bytes 393220
  19.3 17.5 %copy-start.10 = (bf16[256]{0:T(256)(128)(2,1)S(1)}, bf16[256]{0:T(256)(128)(2,1)}, u32[]{:S(2)}) copy-start(bf16[256]{0:T(256)(128)(2,1)} %param.33) | copy-start | bytes 1540
  19.3 17.5 %copy-start.11 = (bf16[256]{0:T(256)(128)(2,1)S(1)}, bf16[256]{0:T(256)(128)(2,1)}, u32[]{:S(2)}) copy-start(bf16[256]{0:T(256)(128)(2,1)} %param.38) | copy-start | bytes 1540
  19.3 313.0 %all-to-all-start = ((bf16[16,2,8,39,256]{4,2,3,1,0:T(8,128)(2,1)}), bf16[16,2,8,39,256]{4,2,3,1,0:T(8,128)(2,1)}, u32[]{:S(2)}, u32[]{:S(2)}) async-start(bf16[16,2,8,39,256]{4,2,3,1,0:T(8,128)(2,1)} %stack.2), calls=%async_computation | async-start | bytes 10223616 | tf_op jit(solution)/shard_map/all_to_all | solution.py:80
  34.7 276.2 %all-gather.2.cloned.1.call-start = ((), (), s32[]{:S(2)}) async-start(), calls=%async_computation.1 | async-start | bytes 5431296 | tf_op jit(solution)/shard_map/all_gather | solution.py:78
  324.3 4.7 %copy-start.1 = (f32[2,8,8,39,624]{4,3,2,1,0:T(8,128)}, f32[2,8,8,39,624]{4,3,2,1,0:T(8,128)S(1)}, u32[]{:S(2)}) copy-start(f32[2,8,8,39,624]{4,3,2,1,0:T(8,128)S(1)} %get-tuple-element.161) | copy-start | bytes 37380100
  369.0 10.0 %copy-start.2 = (bf16[2,8,39,256]{3,1,2,0:T(8,128)(2,1)S(1)}, bf16[2,8,39,256]{3,1,2,0:T(8,128)(2,1)}, u32[]{:S(2)}) copy-start(bf16[2,8,39,256]{3,1,2,0:T(8,128)(2,1)} %param.23) | copy-start | bytes 958468
  369.0 10.0 %copy-start.4 = (bf16[256,256]{1,0:T(8,128)(2,1)S(1)}, bf16[256,256]{1,0:T(8,128)(2,1)}, u32[]{:S(2)}) copy-start(bf16[256,256]{1,0:T(8,128)(2,1)} %param.32) | copy-start | bytes 393220
  369.0 11.8 %copy-start.8 = (bf16[256,256]{1,0:T(8,128)(2,1)S(1)}, bf16[256,256]{1,0:T(8,128)(2,1)}, u32[]{:S(2)}) copy-start(bf16[256,256]{1,0:T(8,128)(2,1)} %param.34) | copy-start | bytes 393220
  369.0 11.8 %copy-start.9 = (f32[256]{0:T(256)S(1)}, f32[256]{0:T(256)}, u32[]{:S(2)}) copy-start(f32[256]{0:T(256)} %param.35) | copy-start | bytes 3076
  378.9 2.3 copy-start.7
  387.1 6.8 %collective-permute-start = (bf16[2,39,256]{2,1,0:T(8,128)(2,1)S(1)}, bf16[2,39,256]{2,1,0:T(8,128)(2,1)S(1)}, u32[]{:S(2)}, u32[]{:S(2)}) collective-permute-start(bf16[2,39,256]{2,1,0:T(8,128)(2,1)S(1)} %fusion.50), channel_id=1, source_target_pairs={{0,4},{4,8},{8,12},{12,16},{16,20},{20,24},{24,28},{1,5},{5,9},{9,... | collective-permute-start | bytes 119816 | tf_op jit(solution)/shard_map/while/body/eval_jaxpr/ppermute | solution.py:12
  394.0 6.8 %collective-permute-start = (bf16[2,39,256]{2,1,0:T(8,128)(2,1)S(1)}, bf16[2,39,256]{2,1,0:T(8,128)(2,1)S(1)}, u32[]{:S(2)}, u32[]{:S(2)}) collective-permute-start(bf16[2,39,256]{2,1,0:T(8,128)(2,1)S(1)} %fusion.50), channel_id=1, source_target_pairs={{0,4},{4,8},{8,12},{12,16},{16,20},{20,24},{24,28},{1,5},{5,9},{9,... | collective-permute-start | bytes 119816 | tf_op jit(solution)/shard_map/while/body/eval_jaxpr/ppermute | solution.py:12
  400.8 6.8 %collective-permute-start = (bf16[2,39,256]{2,1,0:T(8,128)(2,1)S(1)}, bf16[2,39,256]{2,1,0:T(8,128)(2,1)S(1)}, u32[]{:S(2)}, u32[]{:S(2)}) collective-permute-start(bf16[2,39,256]{2,1,0:T(8,128)(2,1)S(1)} %fusion.50), channel_id=1, source_target_pairs={{0,4},{4,8},{8,12},{12,16},{16,20},{20,24},{24,28},{1,5},{5,9},{9,... | collective-permute-start | bytes 119816 | tf_op jit(solution)/shard_map/while/body/eval_jaxpr/ppermute | solution.py:12
  407.6 7.2 %collective-permute-start = (bf16[2,39,256]{2,1,0:T(8,128)(2,1)S(1)}, bf16[2,39,256]{2,1,0:T(8,128)(2,1)S(1)}, u32[]{:S(2)}, u32[]{:S(2)}) collective-permute-start(bf16[2,39,256]{2,1,0:T(8,128)(2,1)S(1)} %fusion.50), channel_id=1, source_target_pairs={{0,4},{4,8},{8,12},{12,16},{16,20},{20,24},{24,28},{1,5},{5,9},{9,... | collective-permute-start | bytes 119816 | tf_op jit(solution)/shard_map/while/body/eval_jaxpr/ppermute | solution.py:12
  414.9 6.8 %collective-permute-start = (bf16[2,39,256]{2,1,0:T(8,128)(2,1)S(1)}, bf16[2,39,256]{2,1,0:T(8,128)(2,1)S(1)}, u32[]{:S(2)}, u32[]{:S(2)}) collective-permute-start(bf16[2,39,256]{2,1,0:T(8,128)(2,1)S(1)} %fusion.50), channel_id=1, source_target_pairs={{0,4},{4,8},{8,12},{12,16},{16,20},{20,24},{24,28},{1,5},{5,9},{9,... | collective-permute-start | bytes 119816 | tf_op jit(solution)/shard_map/while/body/eval_jaxpr/ppermute | solution.py:12
  421.7 6.8 %collective-permute-start = (bf16[2,39,256]{2,1,0:T(8,128)(2,1)S(1)}, bf16[2,39,256]{2,1,0:T(8,128)(2,1)S(1)}, u32[]{:S(2)}, u32[]{:S(2)}) collective-permute-start(bf16[2,39,256]{2,1,0:T(8,128)(2,1)S(1)} %fusion.50), channel_id=1, source_target_pairs={{0,4},{4,8},{8,12},{12,16},{16,20},{20,24},{24,28},{1,5},{5,9},{9,... | collective-permute-start | bytes 119816 | tf_op jit(solution)/shard_map/while/body/eval_jaxpr/ppermute | solution.py:12
  428.6 6.8 %collective-permute-start = (bf16[2,39,256]{2,1,0:T(8,128)(2,1)S(1)}, bf16[2,39,256]{2,1,0:T(8,128)(2,1)S(1)}, u32[]{:S(2)}, u32[]{:S(2)}) collective-permute-start(bf16[2,39,256]{2,1,0:T(8,128)(2,1)S(1)} %fusion.50), channel_id=1, source_target_pairs={{0,4},{4,8},{8,12},{12,16},{16,20},{20,24},{24,28},{1,5},{5,9},{9,... | collective-permute-start | bytes 119816 | tf_op jit(solution)/shard_map/while/body/eval_jaxpr/ppermute | solution.py:12
  436.8 0.8 copy-start.3
Sparse Core Ops, SparseCore 0:
  37.6 273.2 all-gather.1
